TPU v7x, 32 devices: a whole 2x2x4 slice. The times are simulated.
32 devices in a mesh: row: 4 (over y, core), col: 8 (over z, x).
Axes of the slice: x: 2, y: 2, z: 4, core: 2. Of those that a mesh axis runs over, the one named last changes fastest.
Arguments:
- tokens: bfloat16 [128, 128, 192], P('row', 'col'), may hold values from -6 to 6
- tissue: int32 [128, 128], P('row', 'col'), may hold values 0 or 1
- ln_gain: float32 [192], replicated, may hold values from 0.5 to 1.5
- in_weight: bfloat16 [192, 768], replicated, may hold values from -0.4375 to 0.4375
- conv_weight: bfloat16 [3, 3, 384], replicated, may hold values from -2 to 2
- conv_bias: float32 [384], replicated, may hold values from -3 to 3
- proj_weight: bfloat16 [4, 384, 44], replicated, may hold values from -0.3125 to 0.3125
- dt_weight: bfloat16 [4, 12, 384], replicated, may hold values from -1.75 to 1.75
- dt_bias: float32 [4, 384], replicated, may hold values from -4 to -1
- a_rate: float32 [4, 384, 16], replicated, may hold values from 0.001 to 1
- skip_d: float32 [4, 384], replicated, may hold values from 0.5 to 1.5
- out_gain: float32 [384], replicated, may hold values from 0.5 to 1.5
- out_weight: bfloat16 [384, 192], replicated, may hold values from -0.3125 to 0.3125
Outputs:
- result: bfloat16 [128, 128, 192], P('row', 'col')
Inputs may be any that keep to these rules, and one draw needn't show every extreme that they name: 1 marks a tissue token, 0 a background token.
All inputs are finite; a program needn't handle non-finite values. No bound on the sum of `tissue` on one device may be relied on, other than what follows from the above.
Results may differ from a plain program's by a relative error of at most 0.0055.
Values may be sent and summed in bfloat16 or wider, within the bound.
A program may use at most 256 MiB of HBM per device.

v0:
```python
import functools
import math

import jax
import jax.numpy as jnp
from jax import lax
from jax.experimental import pallas as pl
from jax.experimental.pallas import tpu as pltpu
from jax.sharding import PartitionSpec as P

LANES = 128
GROUP = 8
STAGGER = 3
SPAN = 4
MESH = pl.DeviceIdType.MESH


def scan_kernel(
    rows, cols, x_ref, gate_ref, tok_ref, tis_ref, proj_ref, dtw_ref, dtb_ref, rate_ref, skip_ref,
    og_ref, ow_ref, out_ref, xs, dl, pj, ys, st, sbuf, rbuf, ssem, rsem
):
    nrow, ncol = lax.axis_size("row"), lax.axis_size("col")
    me_row, me_col = lax.axis_index("row"), lax.axis_index("col")
    count, inner = x_ref.shape
    tiles = inner // LANES
    rank = dtw_ref.shape[1]
    nstate = rate_ref.shape[1]

    barrier = pltpu.get_barrier_semaphore()
    near = (
        (me_col > 0, (me_row, me_col - 1)),
        (me_col < ncol - 1, (me_row, me_col + 1)),
        (me_row > 0, (me_row - 1, me_col)),
        (me_row < nrow - 1, (me_row + 1, me_col)),
    )
    expected = 0
    for there, device in near:
        expected = expected + there.astype(jnp.int32)

        @pl.when(there)
        def _():
            pl.semaphore_signal(barrier, inc=1, device_id=device, device_id_type=MESH)

    pl.semaphore_wait(barrier, expected)

    step = min(count, 128)

    def prepare(c, _):
        at = pl.ds(pl.multiple_of(c * step, step), step)
        block = x_ref[at, :]
        wide = block.astype(jnp.float32)
        mask = tis_ref[at, :]
        skip = jnp.sum(skip_ref[...], axis=0, keepdims=True)
        base = wide * skip
        for e in range(tiles):
            xs[e, at, :] = wide[:, e * LANES : (e + 1) * LANES]
            ys[e, at, :] = base[:, e * LANES : (e + 1) * LANES]
        for k in range(4):
            p = jnp.dot(block, proj_ref[k], preferred_element_type=jnp.float32)
            pj[k, at, : p.shape[1]] = p
            low = p[:, :rank].astype(jnp.bfloat16)
            z = jnp.dot(low, dtw_ref[k], preferred_element_type=jnp.float32) + dtb_ref[k : k + 1, :]
            delta = (jnp.maximum(z, 0.0) + jnp.log1p(jnp.exp(-jnp.abs(z)))) * mask
            for e in range(tiles):
                dl[k * tiles + e, at, :] = delta[:, e * LANES : (e + 1) * LANES]
        return 0

    lax.fori_loop(0, count // step, prepare, 0)

    row_units, col_units = rows // GROUP * tiles, cols // GROUP * tiles
    plans = (
        (0, me_col, (me_row, me_col + 1), ncol, row_units, 0),
        (2, ncol - 1 - me_col, (me_row, me_col - 1), ncol, row_units, row_units),
        (1, me_row, (me_row + 1, me_col), nrow, col_units, 2 * row_units),
        (3, nrow - 1 - me_row, (me_row - 1, me_col), nrow, col_units, 2 * row_units + col_units),
    )

    def copy_of(u, device):
        return pltpu.make_async_remote_copy(
            src_ref=sbuf.at[u],
            dst_ref=rbuf.at[u],
            send_sem=ssem.at[u],
            recv_sem=rsem.at[u],
            device_id=device,
            device_id_type=MESH,
        )

    def unit(k, ahead, device, size, first, q):
        g = q // tiles
        e = q % tiles
        u = first + q
        length = cols if k % 2 == 0 else rows

        @pl.when(ahead > 0)
        def _():
            copy_of(u, device).wait_recv()
            st[...] = rbuf[u].astype(jnp.float32)

        @pl.when(ahead == 0)
        def _():
            st[...] = jnp.zeros_like(st)

        rates = [
            jnp.broadcast_to(
                rate_ref[k, n : n + 1, pl.ds(pl.multiple_of(e * LANES, LANES), LANES)],
                (GROUP, LANES),
            )
            for n in range(nstate)
        ]
        lane = k * tiles + e

        def advance(block, state):
            state = list(state)
            for sub in range(SPAN):
                t = block * SPAN + sub
                if k >= 2:
                    t = length - 1 - t
                if k % 2 == 0:
                    at = pl.ds(g * (GROUP * cols) + t, GROUP, stride=cols)
                else:
                    at = pl.ds(pl.multiple_of(t * cols + g * GROUP, GROUP), GROUP)
                d = dl[lane, at, :]
                dx = d * xs[e, at, :]
                p = pj[k, at, :]
                parts = [None] * 4
                for n in range(nstate):
                    b = jnp.broadcast_to(p[:, rank + n : rank + n + 1], (GROUP, LANES))
                    r = jnp.broadcast_to(
                        p[:, rank + nstate + n : rank + nstate + n + 1], (GROUP, LANES)
                    )
                    state[n] = jnp.exp2(d * rates[n]) * state[n] + dx * b
                    term = state[n] * r
                    parts[n % 4] = term if parts[n % 4] is None else parts[n % 4] + term
                ys[e, at, :] += (parts[0] + parts[1]) + (parts[2] + parts[3])
            return tuple(state)

        state = tuple(st[n * GROUP : (n + 1) * GROUP, :] for n in range(nstate))
        state = lax.fori_loop(0, length // SPAN, advance, state)

        @pl.when(ahead < size - 1)
        def _():
            sbuf[u] = jnp.concatenate(state, axis=0).astype(jnp.bfloat16)
            copy_of(u, device).start()

    slots = max(STAGGER * (ncol - 1) + row_units, STAGGER * (nrow - 1) + col_units)

    def slot(s, _):
        for k, ahead, device, size, units, first in plans:
            q = s - STAGGER * ahead

            @pl.when((q >= 0) & (q < units))
            def _():
                unit(k, ahead, device, size, first, q)

        return 0

    lax.fori_loop(0, slots, slot, 0)

    def finish(c, _):
        at = pl.ds(pl.multiple_of(c * step, step), step)
        parts = [ys[e, at, :] for e in range(tiles)]
        mean = sum(jnp.sum(a, axis=1, keepdims=True) for a in parts) / inner
        parts = [a - mean for a in parts]
        spread = sum(jnp.sum(a * a, axis=1, keepdims=True) for a in parts) / inner
        scale = lax.rsqrt(spread + 1e-05)
        gate = gate_ref[at, :].astype(jnp.float32)
        gate = gate * jax.nn.sigmoid(gate) * og_ref[...]
        mixed = (jnp.concatenate(parts, axis=1) * scale * gate).astype(jnp.bfloat16)
        branch = jnp.dot(mixed, ow_ref[...], preferred_element_type=jnp.float32)
        out_ref[at, :] = (tok_ref[at, :].astype(jnp.float32) + tis_ref[at, :] * branch).astype(
            jnp.bfloat16
        )
        return 0

    lax.fori_loop(0, count // step, finish, 0)

    for k, ahead, device, size, units, first in plans:

        @pl.when(ahead < size - 1)
        def _():
            def drain(q, _):
                copy_of(first + q, device).wait_send()
                return 0

            lax.fori_loop(0, units, drain, 0)


def mix(x, gate, tokens, tissue, proj, dtw, dtb, rate, skip, og, ow, rows, cols):
    count, inner = x.shape
    tiles = inner // LANES
    nstate = rate.shape[1]
    units = 2 * tiles * (rows // GROUP + cols // GROUP)
    held = (units, nstate * GROUP, LANES)
    return pl.pallas_call(
        functools.partial(scan_kernel, rows, cols),
        out_shape=jax.ShapeDtypeStruct((count, ow.shape[1]), jnp.bfloat16),
        in_specs=[pl.BlockSpec(memory_space=pltpu.VMEM)] * 11,
        out_specs=pl.BlockSpec(memory_space=pltpu.VMEM),
        scratch_shapes=[
            pltpu.VMEM((tiles, count, LANES), jnp.float32),
            pltpu.VMEM((4 * tiles, count, LANES), jnp.float32),
            pltpu.VMEM((4, count, LANES), jnp.float32),
            pltpu.VMEM((tiles, count, LANES), jnp.float32),
            pltpu.VMEM((nstate * GROUP, LANES), jnp.float32),
            pltpu.VMEM(held, jnp.bfloat16),
            pltpu.VMEM(held, jnp.bfloat16),
            pltpu.SemaphoreType.DMA((units,)),
            pltpu.SemaphoreType.DMA((units,)),
        ],
        compiler_params=pltpu.CompilerParams(
            collective_id=0, has_side_effects=True, vmem_limit_bytes=40 * 1024 * 1024
        ),
    )(x, gate, tokens, tissue, proj, dtw, dtb, rate, skip, og, ow)


def padded_2(block, sides, width):
    for axis, dim in sides:
        count = lax.axis_size(axis)
        forward = [(i, i + 1) for i in range(count - 1)]
        backward = [(target, source) for source, target in forward]
        low = lax.ppermute(
            lax.slice_in_dim(block, block.shape[dim] - width, None, axis=dim), axis, forward
        )
        high = lax.ppermute(lax.slice_in_dim(block, 0, width, axis=dim), axis, backward)
        block = jnp.concatenate([low, block, high], axis=dim)
    return block


def layer_norm(values, gain):
    center = values - jnp.mean(values, axis=-1, keepdims=True)
    spread = jnp.mean(center * center, axis=-1, keepdims=True)
    return center * lax.rsqrt(spread + 1e-05) * gain


def conv_silu(padded, conv_weight, conv_bias, height, width):
    summed = jnp.broadcast_to(conv_bias, (height, width, conv_bias.shape[0]))
    for offset_row in range(3):
        for offset_col in range(3):
            window = padded[offset_row : offset_row + height, offset_col : offset_col + width]
            summed = summed + window.astype(jnp.float32) * conv_weight[
                offset_row, offset_col
            ].astype(jnp.float32)
    return jax.nn.silu(summed).astype(jnp.bfloat16)


def local(
    tokens,
    tissue,
    ln_gain,
    in_weight,
    conv_weight,
    conv_bias,
    proj_weight,
    dt_weight,
    dt_bias,
    a_rate,
    skip_d,
    out_gain,
    out_weight,
):
    rows_here, cols_here, width = tokens.shape
    inner = in_weight.shape[1] // 2
    normed = layer_norm(tokens.astype(jnp.float32), ln_gain).astype(jnp.bfloat16)
    projected = jnp.dot(
        normed.reshape(rows_here * cols_here, width), in_weight, preferred_element_type=jnp.float32
    )
    projected = projected.astype(jnp.bfloat16).reshape(rows_here, cols_here, 2 * inner)
    inner_part = projected[:, :, :inner]
    gate_part = projected[:, :, inner:]
    padded = padded_2(inner_part, (("row", 0), ("col", 1)), 1)
    conv_out = conv_silu(padded, conv_weight, conv_bias, rows_here, cols_here)
    count = rows_here * cols_here
    out = mix(
        conv_out.reshape(count, inner),
        gate_part.reshape(count, inner),
        tokens.reshape(count, width),
        tissue.astype(jnp.float32).reshape(count, 1),
        proj_weight,
        dt_weight,
        dt_bias,
        a_rate.transpose(0, 2, 1) * (-1.0 / math.log(2.0)),
        skip_d,
        out_gain.reshape(1, inner),
        out_weight,
        rows_here,
        cols_here,
    )
    return out.reshape(rows_here, cols_here, width)


def solution(mesh):
    return jax.shard_map(
        local,
        mesh=mesh,
        in_specs=(
            P("row", "col", None),
            P("row", "col"),
            P(),
            P(),
            P(),
            P(),
            P(),
            P(),
            P(),
            P(),
            P(),
            P(),
            P(),
        ),
        out_specs=P("row", "col", None),
        check_vma=False,
    )
```

profile of v0, /device:TPU:0, one launch (start us, length us, event | category | flops | bytes accessed | tf_op | source)
XLA Modules:
  0.0 110.1 jit_solution(14455729626481112824)
XLA Ops:
  0.0 0.0 copy-start
  0.0 0.0 copy-start.1
  0.0 1.2 %convert_reduce_fusion = f32[32,16]{1,0:T(8,128)S(1)} fusion(bf16[32,16,192]{2,1,0:T(8,128)(2,1)} %param.13), kind=kLoop, calls=%fused_computation.3 | loop fusion | flops 196096 | bytes 198656 | tf_op jit(solution)/shard_map/reduce_sum | solution.py:230
  1.2 1.2 %fusion.2 = f32[32,16]{1,0:T(8,128)S(1)} fusion(bf16[32,16,192]{2,1,0:T(8,128)(2,1)} %param.13, f32[32,16]{1,0:T(8,128)S(1)} %broadcast_multiply_fusion), kind=kLoop, calls=%fused_computation.8 | loop fusion | flops 392704 | bytes 200704 | tf_op jit(solution)/shard_map/reduce_sum | solution.py:231
  2.4 0.0 copy-done.1
  2.4 0.9 fusion.4
  3.3 0.0 copy-done
  3.3 0.4 convolution_convert_fusion
  3.7 2.4 %collective-permute-start = (bf16[1,16,384]{2,1,0:T(8,128)(2,1)S(1)}, bf16[1,16,384]{2,1,0:T(8,128)(2,1)S(1)}, u32[]{:S(2)}, u32[]{:S(2)}) collective-permute-start(bf16[1,16,384]{2,1,0:T(8,128)(2,1)S(1)} %get-tuple-element.16), channel_id=1, source_target_pairs={{0,8},{8,16},{16,24},{1,9},{9,17},{17,25},{2,10},{10,18},{18,26},{... | collective-permute-start | bytes 36872 | tf_op jit(solution)/shard_map/ppermute | solution.py:221
  6.1 0.0 copy-start.6
  6.1 0.0 copy-start.8
  6.1 0.0 copy-start.5
  6.1 1.4 %collective-permute-start.1 = (bf16[1,16,384]{2,1,0:T(8,128)(2,1)S(1)}, bf16[1,16,384]{2,1,0:T(8,128)(2,1)S(1)}, u32[]{:S(2)}, u32[]{:S(2)}) collective-permute-start(bf16[1,16,384]{2,1,0:T(8,128)(2,1)S(1)} %get-tuple-element.17), channel_id=1, source_target_pairs={{8,0},{16,8},{24,16},{9,1},{17,9},{25,17},{10,2},{18,10},{26,18},{... | collective-permute-start | bytes 36872 | tf_op jit(solution)/shard_map/ppermute | solution.py:224
  7.5 0.1 fusion.5
  7.6 0.0 copy-done.6
  7.6 0.0 copy-start.9
  7.6 0.0 copy-start.4
  7.7 0.0 collective-permute-done
  7.7 3.8 %collective-permute-done.1 = bf16[1,16,384]{2,1,0:T(8,128)(2,1)S(1)} collective-permute-done((bf16[1,16,384]{2,1,0:T(8,128)(2,1)S(1)}, bf16[1,16,384]{2,1,0:T(8,128)(2,1)S(1)}, u32[]{:S(2)}, u32[]{:S(2)}) %collective-permute-start.1) | collective-permute-done | bytes 12320 | tf_op jit(solution)/shard_map/ppermute | solution.py:224
  11.4 0.0 copy-start.7
  11.4 0.1 pad_maximum_fusion.5
  11.5 0.0 copy-start.11
  11.5 3.4 %collective-permute-start.2 = (bf16[34,1,384]{2,1,0:T(2,128)(2,1)S(1)}, bf16[34,1,384]{2,1,0:T(2,128)(2,1)S(1)}, u32[]{:S(2)}, u32[]{:S(2)}) collective-permute-start(bf16[34,1,384]{2,1,0:T(2,128)(2,1)S(1)} %get-tuple-element.20), channel_id=1, source_target_pairs={{0,1},{1,2},{2,3},{3,4},{4,5},{5,6},{6,7},{8,9},{9,10},{10,11},{11... | collective-permute-start | bytes 78344 | tf_op jit(solution)/shard_map/ppermute | solution.py:221
  14.9 1.3 %collective-permute-start.3 = (bf16[34,1,384]{2,1,0:T(2,128)(2,1)S(1)}, bf16[34,1,384]{2,1,0:T(2,128)(2,1)S(1)}, u32[]{:S(2)}, u32[]{:S(2)}) collective-permute-start(bf16[34,1,384]{2,1,0:T(2,128)(2,1)S(1)} %get-tuple-element.21), channel_id=1, source_target_pairs={{1,0},{2,1},{3,2},{4,3},{5,4},{6,5},{7,6},{9,8},{10,9},{11,10},{12... | collective-permute-start | bytes 78344 | tf_op jit(solution)/shard_map/ppermute | solution.py:224
  16.2 0.0 copy-done.8
  16.2 0.1 convert_reduce_fusion.9
  16.3 0.0 copy-done.5
  16.3 0.3 copy.20.proj_ref
  16.6 0.0 copy-done.9
  16.6 0.1 copy.18
  16.7 0.2 reshape.54.tis_ref
  16.9 0.0 copy-done.4
  16.9 0.1 copy.22.ow_ref
  17.0 0.0 copy-done.7
  17.0 0.0 copy-done.11
  17.1 0.0 copy-start.10
  17.1 0.0 collective-permute-done.2
  17.1 3.9 %collective-permute-done.3 = bf16[34,1,384]{2,1,0:T(2,128)(2,1)S(1)} collective-permute-done((bf16[34,1,384]{2,1,0:T(2,128)(2,1)S(1)}, bf16[34,1,384]{2,1,0:T(2,128)(2,1)S(1)}, u32[]{:S(2)}, u32[]{:S(2)}) %collective-permute-start.3) | collective-permute-done | bytes 26144 | tf_op jit(solution)/shard_map/ppermute | solution.py:224
  21.0 0.3 maximum_maximum_fusion
  21.3 0.0 copy-done.10
  21.3 0.0 copy-start.2
  21.3 0.0 copy-start.3
  21.3 0.8 multiply_convert_fusion
  22.1 0.0 copy-done.2
  22.1 0.0 copy-done.3
  22.2 87.2 %shard_map.127 = bf16[512,192]{1,0:T(8,128)(2,1)S(1)} custom-call(bf16[512,384]{1,0:T(8,128)(2,1)S(1)} %bitcast.11, bf16[512,384]{1,0:T(8,128)(2,1)S(1)} %bitcast.12, bf16[512,192]{1,0:T(8,128)(2,1)S(1)} %bitcast.10, f32[512,1]{1,0:T(8,128)S(1)} %reshape.54.tis_ref, bf16[4,384,44]{2,1,0:T(8,128)(2,1)S(1)} %copy.20.proj_ref, ...), custom_call_target="tpu_custom_call" | custom-call | tf_op jit(solution)/shard_map/pallas_call | solution.py:194
  109.4 0.7 copy.24
  (7 shorter events, 0.0 us)
Async XLA Ops:
  0.0 3.3 %copy-start = (bf16[192,768]{1,0:T(8,128)(2,1)S(1)}, bf16[192,768]{1,0:T(8,128)(2,1)}, u32[]{:S(2)}) copy-start(bf16[192,768]{1,0:T(8,128)(2,1)} %param.16) | copy-start | bytes 884740
  0.0 2.4 %copy-start.1 = (bf16[32,16,192]{2,1,0:T(8,128)(2,1)S(1)}, bf16[32,16,192]{2,1,0:T(8,128)(2,1)}, u32[]{:S(2)}) copy-start(bf16[32,16,192]{2,1,0:T(8,128)(2,1)} %param.13) | copy-start | bytes 589828
  3.7 4.0 %collective-permute-start = (bf16[1,16,384]{2,1,0:T(8,128)(2,1)S(1)}, bf16[1,16,384]{2,1,0:T(8,128)(2,1)S(1)}, u32[]{:S(2)}, u32[]{:S(2)}) collective-permute-start(bf16[1,16,384]{2,1,0:T(8,128)(2,1)S(1)} %get-tuple-element.16), channel_id=1, source_target_pairs={{0,8},{8,16},{16,24},{1,9},{9,17},{17,25},{2,10},{10,18},{18,26},{... | collective-permute-start | bytes 36872 | tf_op jit(solution)/shard_map/ppermute | solution.py:221
  6.1 1.6 %copy-start.6 = (f32[4,384,16]{1,2,0:T(8,128)S(1)}, f32[4,384,16]{1,2,0:T(8,128)}, u32[]{:S(2)}) copy-start(f32[4,384,16]{1,2,0:T(8,128)} %param.22) | copy-start | bytes 294916
  6.1 10.2 %copy-start.8 = (bf16[3,3,384]{2,1,0:T(4,128)(2,1)S(1)}, bf16[3,3,384]{2,1,0:T(4,128)(2,1)}, u32[]{:S(2)}) copy-start(bf16[3,3,384]{2,1,0:T(4,128)(2,1)} %param.17) | copy-start | bytes 20740
  6.1 10.2 %copy-start.5 = (bf16[4,384,44]{1,0,2:T(4,128)(2,1)S(1)}, bf16[4,384,44]{1,0,2:T(4,128)(2,1)}, u32[]{:S(2)}) copy-start(bf16[4,384,44]{1,0,2:T(4,128)(2,1)} %param.19) | copy-start | bytes 405508
  6.1 5.3 %collective-permute-start.1 = (bf16[1,16,384]{2,1,0:T(8,128)(2,1)S(1)}, bf16[1,16,384]{2,1,0:T(8,128)(2,1)S(1)}, u32[]{:S(2)}, u32[]{:S(2)}) collective-permute-start(bf16[1,16,384]{2,1,0:T(8,128)(2,1)S(1)} %get-tuple-element.17), channel_id=1, source_target_pairs={{8,0},{16,8},{24,16},{9,1},{17,9},{25,17},{10,2},{18,10},{26,18},{... | collective-permute-start | bytes 36872 | tf_op jit(solution)/shard_map/ppermute | solution.py:224
  7.6 9.0 %copy-start.9 = (s32[32,16]{0,1:T(8,128)S(1)}, s32[32,16]{0,1:T(8,128)}, u32[]{:S(2)}) copy-start(s32[32,16]{0,1:T(8,128)} %param.14) | copy-start | bytes 6148
  7.6 9.2 %copy-start.4 = (bf16[384,192]{0,1:T(8,128)(2,1)S(1)}, bf16[384,192]{0,1:T(8,128)(2,1)}, u32[]{:S(2)}) copy-start(bf16[384,192]{0,1:T(8,128)(2,1)} %param.25) | copy-start | bytes 442372
  11.4 5.6 %copy-start.7 = (bf16[4,12,384]{2,0,1:T(4,128)(2,1)S(1)}, bf16[4,12,384]{2,0,1:T(4,128)(2,1)}, u32[]{:S(2)}) copy-start(bf16[4,12,384]{2,0,1:T(4,128)(2,1)} %param.20) | copy-start | bytes 110596
  11.5 5.5 %copy-start.11 = (f32[384]{0:T(512)S(1)}, f32[384]{0:T(512)}, u32[]{:S(2)}) copy-start(f32[384]{0:T(512)} %param.24) | copy-start | bytes 4612
  11.5 5.5 %collective-permute-start.2 = (bf16[34,1,384]{2,1,0:T(2,128)(2,1)S(1)}, bf16[34,1,384]{2,1,0:T(2,128)(2,1)S(1)}, u32[]{:S(2)}, u32[]{:S(2)}) collective-permute-start(bf16[34,1,384]{2,1,0:T(2,128)(2,1)S(1)} %get-tuple-element.20), channel_id=1, source_target_pairs={{0,1},{1,2},{2,3},{3,4},{4,5},{5,6},{6,7},{8,9},{9,10},{10,11},{11... | collective-permute-start | bytes 78344 | tf_op jit(solution)/shard_map/ppermute | solution.py:221
  14.9 6.0 %collective-permute-start.3 = (bf16[34,1,384]{2,1,0:T(2,128)(2,1)S(1)}, bf16[34,1,384]{2,1,0:T(2,128)(2,1)S(1)}, u32[]{:S(2)}, u32[]{:S(2)}) collective-permute-start(bf16[34,1,384]{2,1,0:T(2,128)(2,1)S(1)} %get-tuple-element.21), channel_id=1, source_target_pairs={{1,0},{2,1},{3,2},{4,3},{5,4},{6,5},{7,6},{9,8},{10,9},{11,10},{12... | collective-permute-start | bytes 78344 | tf_op jit(solution)/shard_map/ppermute | solution.py:224
  17.1 4.2 %copy-start.10 = (f32[384]{0:T(512)S(1)}, f32[384]{0:T(512)}, u32[]{:S(2)}) copy-start(f32[384]{0:T(512)} %param.18) | copy-start | bytes 4612
  21.3 0.8 copy-start.2
  21.3 0.8 copy-start.3
where the time goes:
time: 110 us
  Pallas kernels  87.2 us (79%)
  starting transfers between devices  8.47 us (8%)
  waiting for transfers between devices  7.62 us (7%)
  other arithmetic  4.54 us (4%)
  local copies, waits for them, and re-layouts  1.53 us (1%)
    pallas_call x1, Pallas kernels, mix(): pl.pallas_call(functools.partial(scan_kernel, rows, cols), out_shape=jax....  87.2 us
    ppermute x2, waiting for transfers between devices, padded_2(): lax.ppermute(lax.slice_in_dim(block, 0, width, axis=dim), axis, backward)  7.62 us
    ppermute x2, starting transfers between devices, padded_2(): lax.ppermute(lax.slice_in_dim(block, block.shape[dim] - width, None, axis...  5.75 us
    ppermute x2, starting transfers between devices, padded_2(): lax.ppermute(lax.slice_in_dim(block, 0, width, axis=dim), axis, backward)  2.72 us
  transfers between devices with their start and end apart: 4, of which 2 were waited for; matrix products, arithmetic and copies ran while one was open for 1% of the time, Pallas kernels for 0%

commit v1 on v0

--- a/solution.py
+++ b/solution.py
@@ -15,9 +15,46 @@
 MESH = pl.DeviceIdType.MESH
 
 
+def spread_out(rows, cols, rank, nstate, pj, pk, ex):
+    count = rows * cols
+
+    def reorder(i, _):
+        t, g = i // (rows // GROUP), i % (rows // GROUP)
+        source = pl.ds(g * (GROUP * cols) + t, GROUP, stride=cols)
+        target = pl.ds(pl.multiple_of(t * rows + g * GROUP, GROUP), GROUP)
+        for k in (0, 2):
+            ex[k, 0, target, :] = pj[k, source, :]
+        return 0
+
+    lax.fori_loop(0, count // GROUP, reorder, 0)
+    for k in range(4):
+        for c in range(count // 128):
+            at = pl.ds(c * 128, 128)
+            value = pj[k, at, :] if k % 2 else ex[k, 0, at, :]
+            high = value.astype(jnp.bfloat16)
+            low = (value - high.astype(jnp.float32)).astype(jnp.bfloat16)
+            pk[k, at, :LANES] = high
+            pk[k, at, LANES:] = low
+
+    source = lax.broadcasted_iota(jnp.int32, (2 * LANES, 2 * LANES), 0) % LANES
+    target = lax.broadcasted_iota(jnp.int32, (2 * LANES, 2 * LANES), 1) // LANES
+
+    def pair(m, _):
+        pick = (source == target + (rank + 2 * m)).astype(jnp.bfloat16)
+        for k in range(4):
+            for c in range(count // 256):
+                at = pl.ds(c * 256, 256)
+                value = jnp.dot(pk[k, at, :], pick, preferred_element_type=jnp.float32)
+                ex[k, 2 * m, at, :] = value[:, :LANES]
+                ex[k, 2 * m + 1, at, :] = value[:, LANES:]
+        return 0
+
+    lax.fori_loop(0, nstate, pair, 0)
+
+
 def scan_kernel(
     rows, cols, x_ref, gate_ref, tok_ref, tis_ref, proj_ref, dtw_ref, dtb_ref, rate_ref, skip_ref,
-    og_ref, ow_ref, out_ref, xs, dl, pj, ys, st, sbuf, rbuf, ssem, rsem
+    og_ref, ow_ref, out_ref, xs, dl, pj, ys, st, sbuf, rbuf, ssem, rsem, *wide_refs
 ):
     nrow, ncol = lax.axis_size("row"), lax.axis_size("col")
     me_row, me_col = lax.axis_index("row"), lax.axis_index("col")
@@ -57,7 +94,9 @@
             ys[e, at, :] = base[:, e * LANES : (e + 1) * LANES]
         for k in range(4):
             p = jnp.dot(block, proj_ref[k], preferred_element_type=jnp.float32)
-            pj[k, at, : p.shape[1]] = p
+            pj[k, at, :] = jnp.concatenate(
+                [p, jnp.zeros((step, LANES - p.shape[1]), jnp.float32)], axis=1
+            )
             low = p[:, :rank].astype(jnp.bfloat16)
             z = jnp.dot(low, dtw_ref[k], preferred_element_type=jnp.float32) + dtb_ref[k : k + 1, :]
             delta = (jnp.maximum(z, 0.0) + jnp.log1p(jnp.exp(-jnp.abs(z)))) * mask
@@ -67,6 +106,8 @@
 
     lax.fori_loop(0, count // step, prepare, 0)
 
+    if wide_refs:
+        spread_out(rows, cols, rank, nstate, pj, *wide_refs)
     row_units, col_units = rows // GROUP * tiles, cols // GROUP * tiles
     plans = (
         (0, me_col, (me_row, me_col + 1), ncol, row_units, 0),
@@ -121,15 +162,22 @@
                     at = pl.ds(pl.multiple_of(t * cols + g * GROUP, GROUP), GROUP)
                 d = dl[lane, at, :]
                 dx = d * xs[e, at, :]
-                p = pj[k, at, :]
+                if wide_refs:
+                    ex = wide_refs[1]
+                    where = at
+                    if k % 2 == 0:
+                        where = pl.ds(pl.multiple_of(t * rows + g * GROUP, GROUP), GROUP)
+                    wide = [ex[k, m, where, :] for m in range(2 * nstate)]
+                else:
+                    p = pj[k, at, :]
+                    wide = [
+                        jnp.broadcast_to(p[:, rank + m : rank + m + 1], (GROUP, LANES))
+                        for m in range(2 * nstate)
+                    ]
                 parts = [None] * 4
                 for n in range(nstate):
-                    b = jnp.broadcast_to(p[:, rank + n : rank + n + 1], (GROUP, LANES))
-                    r = jnp.broadcast_to(
-                        p[:, rank + nstate + n : rank + nstate + n + 1], (GROUP, LANES)
-                    )
-                    state[n] = jnp.exp2(d * rates[n]) * state[n] + dx * b
-                    term = state[n] * r
+                    state[n] = jnp.exp2(d * rates[n]) * state[n] + dx * wide[n]
+                    term = state[n] * wide[nstate + n]
                     parts[n % 4] = term if parts[n % 4] is None else parts[n % 4] + term
                 ys[e, at, :] += (parts[0] + parts[1]) + (parts[2] + parts[3])
             return tuple(state)
@@ -190,6 +238,12 @@
     tiles = inner // LANES
     nstate = rate.shape[1]
     units = 2 * tiles * (rows // GROUP + cols // GROUP)
+    wide_shapes = []
+    if count <= 512 and count % 256 == 0:
+        wide_shapes = [
+            pltpu.VMEM((4, count, 2 * LANES), jnp.bfloat16),
+            pltpu.VMEM((4, 2 * nstate, count, LANES), jnp.float32),
+        ]
     held = (units, nstate * GROUP, LANES)
     return pl.pallas_call(
         functools.partial(scan_kernel, rows, cols),
@@ -206,9 +260,10 @@
             pltpu.VMEM(held, jnp.bfloat16),
             pltpu.SemaphoreType.DMA((units,)),
             pltpu.SemaphoreType.DMA((units,)),
+            *wide_shapes,
         ],
         compiler_params=pltpu.CompilerParams(
-            collective_id=0, has_side_effects=True, vmem_limit_bytes=40 * 1024 * 1024
+            collective_id=0, has_side_effects=True, vmem_limit_bytes=56 * 1024 * 1024
         ),
     )(x, gate, tokens, tissue, proj, dtw, dtb, rate, skip, og, ow)
 

time: 110 us -> 89 us (0.81)
  Pallas kernels: 87.2 us -> 64.1 us
  local copies, waits for them, and re-layouts: 1.53 us -> 6.48 us
  waiting for transfers between devices: 7.62 us -> 3.12 us
  other arithmetic: 4.54 us -> 5.92 us
    pallas_call x1, Pallas kernels: 87.2 us -> 64.1 us  [mix(): pl.pallas_call(functools.partial(scan_kernel, rows, cols), out_shape=jax....]
    ppermute x2, waiting for transfers between devices: 7.62 us -> 3.11 us  [padded_2(): lax.ppermute(lax.slice_in_dim(block, 0, width, axis=dim), axis, backward)]
    unnamed x28 -> x24, local copies, waits for them, and re-layouts: 1.21 us -> 4.17 us
  transfers between devices with their start and end apart: 4 -> 4, of which waited for: 2 -> 2; matrix products, arithmetic and copies ran while one was open for 1% -> 6% of each run, Pallas kernels for 0% -> 0%
where the time goes in v1:
time: 89 us; the launch traced here: 88.6 us
  Pallas kernels  64.1 us (72%)
  starting transfers between devices  8.46 us (10%)
  local copies, waits for them, and re-layouts  6.48 us (7%)
  other arithmetic  5.92 us (7%)
  waiting for transfers between devices  3.12 us (4%)
    pallas_call x1, Pallas kernels, mix(): pl.pallas_call(functools.partial(scan_kernel, rows, cols), out_shape=jax....  64.1 us
    ppermute x2, starting transfers between devices, padded_2(): lax.ppermute(lax.slice_in_dim(block, block.shape[dim] - width, None, axis...  5.75 us
    unnamed x24, local copies, waits for them, and re-layouts  4.17 us
    ppermute x2, waiting for transfers between devices, padded_2(): lax.ppermute(lax.slice_in_dim(block, 0, width, axis=dim), axis, backward)  3.11 us
    ppermute x2, starting transfers between devices, padded_2(): lax.ppermute(lax.slice_in_dim(block, 0, width, axis=dim), axis, backward)  2.72 us
  transfers between devices with their start and end apart: 4, of which 2 were waited for; matrix products, arithmetic and copies ran while one was open for 6% of the time, Pallas kernels for 0%

profile of v1, /device:TPU:0, one launch (start us, length us, event | category | flops | bytes accessed | tf_op | source)
XLA Modules:
  0.0 88.6 jit_solution(5688599275226636332)
XLA Ops:
  0.0 0.0 copy-start
  0.0 0.0 copy-start.1
  0.0 1.2 %convert_reduce_fusion = f32[32,16]{1,0:T(8,128)S(1)} fusion(bf16[32,16,192]{2,1,0:T(8,128)(2,1)} %param.13), kind=kLoop, calls=%fused_computation.3 | loop fusion | flops 196096 | bytes 198656 | tf_op jit(solution)/shard_map/reduce_sum | solution.py:285
  1.2 1.2 %fusion.2 = f32[32,16]{1,0:T(8,128)S(1)} fusion(bf16[32,16,192]{2,1,0:T(8,128)(2,1)} %param.13, f32[32,16]{1,0:T(8,128)S(1)} %broadcast_multiply_fusion), kind=kLoop, calls=%fused_computation.8 | loop fusion | flops 392704 | bytes 200704 | tf_op jit(solution)/shard_map/reduce_sum | solution.py:286
  2.4 0.0 copy-done.1
  2.4 0.9 fusion.4
  3.3 0.0 copy-done
  3.3 0.4 convolution_convert_fusion
  3.7 2.4 %collective-permute-start = (bf16[1,16,384]{2,1,0:T(8,128)(2,1)S(1)}, bf16[1,16,384]{2,1,0:T(8,128)(2,1)S(1)}, u32[]{:S(2)}, u32[]{:S(2)}) collective-permute-start(bf16[1,16,384]{2,1,0:T(8,128)(2,1)S(1)} %get-tuple-element.16), channel_id=1, source_target_pairs={{0,8},{8,16},{16,24},{1,9},{9,17},{17,25},{2,10},{10,18},{18,26},{... | collective-permute-start | bytes 36872 | tf_op jit(solution)/shard_map/ppermute | solution.py:276
  6.1 0.0 copy-start.4
  6.1 0.0 copy-start.6
  6.1 0.0 copy-start.3
  6.1 1.4 %collective-permute-start.1 = (bf16[1,16,384]{2,1,0:T(8,128)(2,1)S(1)}, bf16[1,16,384]{2,1,0:T(8,128)(2,1)S(1)}, u32[]{:S(2)}, u32[]{:S(2)}) collective-permute-start(bf16[1,16,384]{2,1,0:T(8,128)(2,1)S(1)} %get-tuple-element.17), channel_id=1, source_target_pairs={{8,0},{16,8},{24,16},{9,1},{17,9},{25,17},{10,2},{18,10},{26,18},{... | collective-permute-start | bytes 36872 | tf_op jit(solution)/shard_map/ppermute | solution.py:279
  7.5 0.8 fusion.5
  8.3 0.0 copy-done.4
  8.3 0.0 copy-start.7
  8.3 0.0 copy-start.2
  8.3 0.6 multiply_bitcast_fusion.rate_ref
  9.0 0.0 collective-permute-done
  9.0 2.4 %collective-permute-done.1 = bf16[1,16,384]{2,1,0:T(8,128)(2,1)S(1)} collective-permute-done((bf16[1,16,384]{2,1,0:T(8,128)(2,1)S(1)}, bf16[1,16,384]{2,1,0:T(8,128)(2,1)S(1)}, u32[]{:S(2)}, u32[]{:S(2)}) %collective-permute-start.1) | collective-permute-done | bytes 12320 | tf_op jit(solution)/shard_map/ppermute | solution.py:279
  11.4 0.0 copy-start.5
  11.4 0.1 pad_maximum_fusion.5
  11.5 0.0 copy-start.9
  11.5 3.4 %collective-permute-start.2 = (bf16[34,1,384]{2,1,0:T(2,128)(2,1)S(1)}, bf16[34,1,384]{2,1,0:T(2,128)(2,1)S(1)}, u32[]{:S(2)}, u32[]{:S(2)}) collective-permute-start(bf16[34,1,384]{2,1,0:T(2,128)(2,1)S(1)} %get-tuple-element.20), channel_id=1, source_target_pairs={{0,1},{1,2},{2,3},{3,4},{4,5},{5,6},{6,7},{8,9},{9,10},{10,11},{11... | collective-permute-start | bytes 78344 | tf_op jit(solution)/shard_map/ppermute | solution.py:276
  14.9 1.3 %collective-permute-start.3 = (bf16[34,1,384]{2,1,0:T(2,128)(2,1)S(1)}, bf16[34,1,384]{2,1,0:T(2,128)(2,1)S(1)}, u32[]{:S(2)}, u32[]{:S(2)}) collective-permute-start(bf16[34,1,384]{2,1,0:T(2,128)(2,1)S(1)} %get-tuple-element.21), channel_id=1, source_target_pairs={{1,0},{2,1},{3,2},{4,3},{5,4},{6,5},{7,6},{9,8},{10,9},{11,10},{12... | collective-permute-start | bytes 78344 | tf_op jit(solution)/shard_map/ppermute | solution.py:279
  16.2 0.0 copy-done.6
  16.2 0.1 convert_reduce_fusion.9
  16.3 0.0 copy-done.3
  16.3 1.0 %copy.20.proj_ref = bf16[4,384,44]{2,1,0:T(8,128)(2,1)} copy(bf16[4,384,44]{1,0,2:T(4,128)(2,1)S(1)} %copy-done.3) | data formatting | bytes 270336 | tf_op args[6]
  17.3 0.0 copy-done.7
  17.3 0.1 copy.18
  17.4 0.9 reshape.54.tis_ref
  18.3 0.0 copy-done.2
  18.3 0.8 copy.22.ow_ref
  19.1 0.0 copy-done.5
  19.1 0.6 copy.21.dtw_ref
  19.7 0.0 copy-done.9
  19.7 0.5 reshape.43.og_ref
  20.3 0.0 copy-start.8
  20.3 0.0 collective-permute-done.2
  20.3 0.7 collective-permute-done.3
  21.0 0.3 maximum_maximum_fusion
  21.3 0.0 copy-done.8
  21.3 1.5 %multiply_convert_fusion = bf16[32,16,384]{2,1,0:T(8,128)(2,1)} fusion(bf16[32,16,384]{2,1,0:T(8,128)(2,1)S(1)} %get-tuple-element.15, bf16[34,17,384]{2,1,0:T(8,128)(2,1)S(1)} %get-tuple-element.19, bf16[1,16,384]{2,1,0:T(8,128)(2,1)S(1)} %collective-permute-done.1, bf16[34,17,384]{2,1,0:T(8,128)(2,1)S(1)} %get-tuple-element.18, ...), kind=kLoop, calls=%fused_computation.1 | loop fusion | flops 6684672 | bytes 3185664 | tf_op jit(solution)/shard_map/convert_element_type | solution.py:298
  22.9 64.1 %shard_map.127 = bf16[512,192]{1,0:T(8,128)(2,1)} custom-call(bf16[512,384]{1,0:T(8,128)(2,1)} %bitcast.13, bf16[512,384]{1,0:T(8,128)(2,1)} %bitcast.14, bf16[512,192]{1,0:T(8,128)(2,1)} %bitcast.10, f32[512,1]{1,0:T(8,128)} %reshape.54.tis_ref, bf16[4,384,44]{2,1,0:T(8,128)(2,1)} %copy.20.proj_ref, bf16[4,12,384]{2,1,0:T(8,128)(2,1)} %copy.21.dtw_ref, ...), custom_call_target="tpu_custom_call" | custom-call | tf_op jit(solution)/shard_map/pallas_call | solution.py:248
  86.9 1.7 %copy.24 = bf16[32,16,192]{2,1,0:T(8,128)(2,1)} copy(bf16[32,16,192]{2,1,0:T(8,128)(2,1)} %bitcast.15) | data formatting | bytes 393216
  (4 shorter events, 0.0 us)
Async XLA Ops:
  0.0 3.3 %copy-start = (bf16[192,768]{1,0:T(8,128)(2,1)S(1)}, bf16[192,768]{1,0:T(8,128)(2,1)}, u32[]{:S(2)}) copy-start(bf16[192,768]{1,0:T(8,128)(2,1)} %param.16) | copy-start | bytes 884740
  0.0 2.4 %copy-start.1 = (bf16[32,16,192]{2,1,0:T(8,128)(2,1)S(1)}, bf16[32,16,192]{2,1,0:T(8,128)(2,1)}, u32[]{:S(2)}) copy-start(bf16[32,16,192]{2,1,0:T(8,128)(2,1)} %param.13) | copy-start | bytes 589828
  3.7 5.3 %collective-permute-start = (bf16[1,16,384]{2,1,0:T(8,128)(2,1)S(1)}, bf16[1,16,384]{2,1,0:T(8,128)(2,1)S(1)}, u32[]{:S(2)}, u32[]{:S(2)}) collective-permute-start(bf16[1,16,384]{2,1,0:T(8,128)(2,1)S(1)} %get-tuple-element.16), channel_id=1, source_target_pairs={{0,8},{8,16},{16,24},{1,9},{9,17},{17,25},{2,10},{10,18},{18,26},{... | collective-permute-start | bytes 36872 | tf_op jit(solution)/shard_map/ppermute | solution.py:276
  6.1 2.3 %copy-start.4 = (f32[4,384,16]{1,2,0:T(8,128)S(1)}, f32[4,384,16]{1,2,0:T(8,128)}, u32[]{:S(2)}) copy-start(f32[4,384,16]{1,2,0:T(8,128)} %param.22) | copy-start | bytes 294916
  6.1 10.2 %copy-start.6 = (bf16[3,3,384]{2,1,0:T(4,128)(2,1)S(1)}, bf16[3,3,384]{2,1,0:T(4,128)(2,1)}, u32[]{:S(2)}) copy-start(bf16[3,3,384]{2,1,0:T(4,128)(2,1)} %param.17) | copy-start | bytes 20740
  6.1 10.2 %copy-start.3 = (bf16[4,384,44]{1,0,2:T(4,128)(2,1)S(1)}, bf16[4,384,44]{1,0,2:T(4,128)(2,1)}, u32[]{:S(2)}) copy-start(bf16[4,384,44]{1,0,2:T(4,128)(2,1)} %param.19) | copy-start | bytes 405508
  6.1 5.3 %collective-permute-start.1 = (bf16[1,16,384]{2,1,0:T(8,128)(2,1)S(1)}, bf16[1,16,384]{2,1,0:T(8,128)(2,1)S(1)}, u32[]{:S(2)}, u32[]{:S(2)}) collective-permute-start(bf16[1,16,384]{2,1,0:T(8,128)(2,1)S(1)} %get-tuple-element.17), channel_id=1, source_target_pairs={{8,0},{16,8},{24,16},{9,1},{17,9},{25,17},{10,2},{18,10},{26,18},{... | collective-permute-start | bytes 36872 | tf_op jit(solution)/shard_map/ppermute | solution.py:279
  8.3 9.0 %copy-start.7 = (s32[32,16]{0,1:T(8,128)S(1)}, s32[32,16]{0,1:T(8,128)}, u32[]{:S(2)}) copy-start(s32[32,16]{0,1:T(8,128)} %param.14) | copy-start | bytes 6148
  8.3 9.9 %copy-start.2 = (bf16[384,192]{0,1:T(8,128)(2,1)S(1)}, bf16[384,192]{0,1:T(8,128)(2,1)}, u32[]{:S(2)}) copy-start(bf16[384,192]{0,1:T(8,128)(2,1)} %param.25) | copy-start | bytes 442372
  11.4 7.7 %copy-start.5 = (bf16[4,12,384]{2,0,1:T(4,128)(2,1)S(1)}, bf16[4,12,384]{2,0,1:T(4,128)(2,1)}, u32[]{:S(2)}) copy-start(bf16[4,12,384]{2,0,1:T(4,128)(2,1)} %param.20) | copy-start | bytes 110596
  11.5 8.2 %copy-start.9 = (f32[384]{0:T(512)S(1)}, f32[384]{0:T(512)}, u32[]{:S(2)}) copy-start(f32[384]{0:T(512)} %param.24) | copy-start | bytes 4612
  11.5 8.7 %collective-permute-start.2 = (bf16[34,1,384]{2,1,0:T(2,128)(2,1)S(1)}, bf16[34,1,384]{2,1,0:T(2,128)(2,1)S(1)}, u32[]{:S(2)}, u32[]{:S(2)}) collective-permute-start(bf16[34,1,384]{2,1,0:T(2,128)(2,1)S(1)} %get-tuple-element.20), channel_id=1, source_target_pairs={{0,1},{1,2},{2,3},{3,4},{4,5},{5,6},{6,7},{8,9},{9,10},{10,11},{11... | collective-permute-start | bytes 78344 | tf_op jit(solution)/shard_map/ppermute | solution.py:276
  14.9 6.0 %collective-permute-start.3 = (bf16[34,1,384]{2,1,0:T(2,128)(2,1)S(1)}, bf16[34,1,384]{2,1,0:T(2,128)(2,1)S(1)}, u32[]{:S(2)}, u32[]{:S(2)}) collective-permute-start(bf16[34,1,384]{2,1,0:T(2,128)(2,1)S(1)} %get-tuple-element.21), channel_id=1, source_target_pairs={{1,0},{2,1},{3,2},{4,3},{5,4},{6,5},{7,6},{9,8},{10,9},{11,10},{12... | collective-permute-start | bytes 78344 | tf_op jit(solution)/shard_map/ppermute | solution.py:279
  20.3 1.0 %copy-start.8 = (f32[384]{0:T(512)S(1)}, f32[384]{0:T(512)}, u32[]{:S(2)}) copy-start(f32[384]{0:T(512)} %param.18) | copy-start | bytes 4612

commit v2 on v1

--- a/solution.py
+++ b/solution.py
@@ -53,8 +53,9 @@
 
 
 def scan_kernel(
-    rows, cols, x_ref, gate_ref, tok_ref, tis_ref, proj_ref, dtw_ref, dtb_ref, rate_ref, skip_ref,
-    og_ref, ow_ref, out_ref, xs, dl, pj, ys, st, sbuf, rbuf, ssem, rsem, *wide_refs
+    rows, cols, tok_ref, lng_ref, inw_ref, cw_ref, cb_ref, tis_ref, proj_ref, dtw_ref, dtb_ref, rate_ref, skip_ref,
+    og_ref, ow_ref, out_ref,
+    edge, halo, hin, pad, gate_ref, x_ref, hs, hr, xs, dl, pj, ys, st, sbuf, rbuf, ssem, rsem, *wide_refs
 ):
     nrow, ncol = lax.axis_size("row"), lax.axis_size("col")
     me_row, me_col = lax.axis_index("row"), lax.axis_index("col")
@@ -64,23 +65,114 @@
     nstate = rate_ref.shape[1]
 
     barrier = pltpu.get_barrier_semaphore()
-    near = (
-        (me_col > 0, (me_row, me_col - 1)),
-        (me_col < ncol - 1, (me_row, me_col + 1)),
-        (me_row > 0, (me_row - 1, me_col)),
-        (me_row < nrow - 1, (me_row + 1, me_col)),
+    last = count - cols
+    sends = (
+        (1, 0, tok_ref.at[pl.ds(last, cols)], 0, cols),
+        (-1, 0, tok_ref.at[pl.ds(0, cols)], cols, cols),
+        (0, 1, edge.at[1], 2 * cols, rows),
+        (0, -1, edge.at[0], 2 * cols + rows, rows),
+        (1, 1, tok_ref.at[pl.ds(count - 16, 16)], 2 * cols + 2 * rows, 16),
+        (1, -1, tok_ref.at[pl.ds(last, 16)], 2 * cols + 2 * rows + 16, 16),
+        (-1, 1, tok_ref.at[pl.ds(cols - 16, 16)], 2 * cols + 2 * rows + 32, 16),
+        (-1, -1, tok_ref.at[pl.ds(0, 16)], 2 * cols + 2 * rows + 48, 16),
     )
+
+    def there(dr, dc):
+        r, c = me_row + dr, me_col + dc
+        return (r >= 0) & (r < nrow) & (c >= 0) & (c < ncol)
+
     expected = 0
-    for there, device in near:
-        expected = expected + there.astype(jnp.int32)
-
-        @pl.when(there)
-        def _():
-            pl.semaphore_signal(barrier, inc=1, device_id=device, device_id_type=MESH)
+    for dr, dc, _, _, _ in sends:
+        expected = expected + there(dr, dc).astype(jnp.int32)
+
+        @pl.when(there(dr, dc))
+        def _():
+            pl.semaphore_signal(
+                barrier, inc=1, device_id=(me_row + dr, me_col + dc), device_id_type=MESH
+            )
+
+    for side in range(2):
+        want = lax.broadcasted_iota(jnp.int32, (rows, count), 0) * cols + side * (cols - 1)
+        pick = (lax.broadcasted_iota(jnp.int32, (rows, count), 1) == want).astype(jnp.bfloat16)
+        edge[side] = jnp.dot(pick, tok_ref[...], preferred_element_type=jnp.float32).astype(
+            jnp.bfloat16
+        )
 
     pl.semaphore_wait(barrier, expected)
 
+    def border(which):
+        dr, dc, source, start, size = sends[which]
+        return pltpu.make_async_remote_copy(
+            src_ref=source,
+            dst_ref=halo.at[pl.ds(start, size)],
+            send_sem=hs.at[which],
+            recv_sem=hr.at[which],
+            device_id=(me_row + dr, me_col + dc),
+            device_id_type=MESH,
+        )
+
+    for which, (dr, dc, _, _, _) in enumerate(sends):
+
+        @pl.when(there(dr, dc))
+        def _():
+            border(which).start()
+
     step = min(count, 128)
+
+    def normed(block):
+        return layer_norm(block.astype(jnp.float32), lng_ref[...]).astype(jnp.bfloat16)
+
+    def project(c, _):
+        at = pl.ds(pl.multiple_of(c * step, step), step)
+        both = jnp.dot(normed(tok_ref[at, :]), inw_ref[...], preferred_element_type=jnp.float32)
+        both = both.astype(jnp.bfloat16)
+        gate_ref[at, :] = both[:, inner:]
+        part = both[:, :inner].astype(jnp.float32).reshape(step // cols, cols, inner)
+        pad[pl.ds(1 + c * (step // cols), step // cols), GROUP : GROUP + cols, :] = part
+        return 0
+
+    lax.fori_loop(0, count // step, project, 0)
+
+    for which, (dr, dc, _, start, size) in enumerate(sends):
+
+        @pl.when(there(-dr, -dc))
+        def _():
+            border(which).wait_recv()
+
+        @pl.when(jnp.logical_not(there(-dr, -dc)))
+        def _():
+            halo[pl.ds(start, size), :] = jnp.zeros((size, halo.shape[1]), jnp.bfloat16)
+
+    around = jnp.dot(normed(halo[...]), inw_ref[:, :inner], preferred_element_type=jnp.float32)
+    hin[...] = around.astype(jnp.bfloat16).astype(jnp.float32)
+    pad[0, GROUP : GROUP + cols, :] = hin[0:cols, :]
+    pad[rows + 1, GROUP : GROUP + cols, :] = hin[cols : 2 * cols, :]
+    low, high = pl.ds(GROUP - 1, 1), pl.ds(GROUP + cols, 1)
+
+    def sides(r, _):
+        pad[r + 1, low, :] = hin[pl.ds(2 * cols + r, 1), :]
+        pad[r + 1, high, :] = hin[pl.ds(2 * cols + rows + r, 1), :]
+        return 0
+
+    lax.fori_loop(0, rows, sides, 0)
+    corner = 2 * cols + 2 * rows
+    pad[0, low, :] = hin[pl.ds(corner + 15, 1), :]
+    pad[0, high, :] = hin[pl.ds(corner + 16, 1), :]
+    pad[rows + 1, low, :] = hin[pl.ds(corner + 47, 1), :]
+    pad[rows + 1, high, :] = hin[pl.ds(corner + 48, 1), :]
+    taps = cw_ref[...].astype(jnp.float32)
+
+    def filtered(r, _):
+        total = jnp.broadcast_to(cb_ref[...], (cols, inner))
+        for i in range(3):
+            for j in range(3):
+                window = pad[r + i, GROUP - 1 + j : GROUP - 1 + j + cols, :]
+                total = total + window * taps[3 * i + j : 3 * i + j + 1, :]
+        total = total * jax.nn.sigmoid(total)
+        x_ref[pl.ds(pl.multiple_of(r * cols, cols), cols), :] = total.astype(jnp.bfloat16)
+        return 0
+
+    lax.fori_loop(0, rows, filtered, 0)
 
     def prepare(c, _):
         at = pl.ds(pl.multiple_of(c * step, step), step)
@@ -222,6 +314,12 @@
 
     lax.fori_loop(0, count // step, finish, 0)
 
+    for which, (dr, dc, _, _, _) in enumerate(sends):
+
+        @pl.when(there(dr, dc))
+        def _():
+            border(which).wait_send()
+
     for k, ahead, device, size, units, first in plans:
 
         @pl.when(ahead < size - 1)
@@ -233,8 +331,9 @@
             lax.fori_loop(0, units, drain, 0)
 
 
-def mix(x, gate, tokens, tissue, proj, dtw, dtb, rate, skip, og, ow, rows, cols):
-    count, inner = x.shape
+def mix(tokens, gain, inw, taps, bias, tissue, proj, dtw, dtb, rate, skip, og, ow, rows, cols):
+    count, width = tokens.shape
+    inner = inw.shape[1] // 2
     tiles = inner // LANES
     nstate = rate.shape[1]
     units = 2 * tiles * (rows // GROUP + cols // GROUP)
@@ -248,9 +347,17 @@
     return pl.pallas_call(
         functools.partial(scan_kernel, rows, cols),
         out_shape=jax.ShapeDtypeStruct((count, ow.shape[1]), jnp.bfloat16),
-        in_specs=[pl.BlockSpec(memory_space=pltpu.VMEM)] * 11,
+        in_specs=[pl.BlockSpec(memory_space=pltpu.VMEM)] * 13,
         out_specs=pl.BlockSpec(memory_space=pltpu.VMEM),
         scratch_shapes=[
+            pltpu.VMEM((2, rows, width), jnp.bfloat16),
+            pltpu.VMEM((2 * rows + 2 * cols + 64, width), jnp.bfloat16),
+            pltpu.VMEM((2 * rows + 2 * cols + 64, inner), jnp.float32),
+            pltpu.VMEM((rows + 2, cols + 2 * GROUP, inner), jnp.float32),
+            pltpu.VMEM((count, inner), jnp.bfloat16),
+            pltpu.VMEM((count, inner), jnp.bfloat16),
+            pltpu.SemaphoreType.DMA((8,)),
+            pltpu.SemaphoreType.DMA((8,)),
             pltpu.VMEM((tiles, count, LANES), jnp.float32),
             pltpu.VMEM((4 * tiles, count, LANES), jnp.float32),
             pltpu.VMEM((4, count, LANES), jnp.float32),
@@ -265,37 +372,13 @@
         compiler_params=pltpu.CompilerParams(
             collective_id=0, has_side_effects=True, vmem_limit_bytes=56 * 1024 * 1024
         ),
-    )(x, gate, tokens, tissue, proj, dtw, dtb, rate, skip, og, ow)
-
-
-def padded_2(block, sides, width):
-    for axis, dim in sides:
-        count = lax.axis_size(axis)
-        forward = [(i, i + 1) for i in range(count - 1)]
-        backward = [(target, source) for source, target in forward]
-        low = lax.ppermute(
-            lax.slice_in_dim(block, block.shape[dim] - width, None, axis=dim), axis, forward
-        )
-        high = lax.ppermute(lax.slice_in_dim(block, 0, width, axis=dim), axis, backward)
-        block = jnp.concatenate([low, block, high], axis=dim)
-    return block
+    )(tokens, gain, inw, taps, bias, tissue, proj, dtw, dtb, rate, skip, og, ow)
 
 
 def layer_norm(values, gain):
     center = values - jnp.mean(values, axis=-1, keepdims=True)
     spread = jnp.mean(center * center, axis=-1, keepdims=True)
     return center * lax.rsqrt(spread + 1e-05) * gain
-
-
-def conv_silu(padded, conv_weight, conv_bias, height, width):
-    summed = jnp.broadcast_to(conv_bias, (height, width, conv_bias.shape[0]))
-    for offset_row in range(3):
-        for offset_col in range(3):
-            window = padded[offset_row : offset_row + height, offset_col : offset_col + width]
-            summed = summed + window.astype(jnp.float32) * conv_weight[
-                offset_row, offset_col
-            ].astype(jnp.float32)
-    return jax.nn.silu(summed).astype(jnp.bfloat16)
 
 
 def local(
@@ -315,20 +398,13 @@
 ):
     rows_here, cols_here, width = tokens.shape
     inner = in_weight.shape[1] // 2
-    normed = layer_norm(tokens.astype(jnp.float32), ln_gain).astype(jnp.bfloat16)
-    projected = jnp.dot(
-        normed.reshape(rows_here * cols_here, width), in_weight, preferred_element_type=jnp.float32
-    )
-    projected = projected.astype(jnp.bfloat16).reshape(rows_here, cols_here, 2 * inner)
-    inner_part = projected[:, :, :inner]
-    gate_part = projected[:, :, inner:]
-    padded = padded_2(inner_part, (("row", 0), ("col", 1)), 1)
-    conv_out = conv_silu(padded, conv_weight, conv_bias, rows_here, cols_here)
     count = rows_here * cols_here
     out = mix(
-        conv_out.reshape(count, inner),
-        gate_part.reshape(count, inner),
         tokens.reshape(count, width),
+        ln_gain.reshape(1, width),
+        in_weight,
+        conv_weight.reshape(9, inner),
+        conv_bias.reshape(1, inner),
         tissue.astype(jnp.float32).reshape(count, 1),
         proj_weight,
         dt_weight,

time: 89 us -> 81.4 us (0.915)
  starting transfers between devices: 8.46 us -> 0 us
  Pallas kernels: 64.1 us -> 69.9 us
  other arithmetic: 5.92 us -> 1.35 us
  local copies, waits for them, and re-layouts: 6.48 us -> 9.79 us
  waiting for transfers between devices: 3.12 us -> 0 us
    ppermute x4 -> x0, starting transfers between devices: 8.46 us -> none  [the longest x2 5.75 us: padded_2(): lax.ppermute(lax.slice_in_dim(block, block.shape[dim] - width, None, axis...]
    pallas_call x1, Pallas kernels: 64.1 us -> 69.9 us  [mix(): pl.pallas_call(functools.partial(scan_kernel, rows, cols), out_shape=jax....]
    ppermute x4 -> x0, waiting for transfers between devices: 3.12 us -> none  [the longest x2 3.11 us: padded_2(): lax.ppermute(lax.slice_in_dim(block, 0, width, axis=dim), axis, backward)]
    reshape x0 -> x2, local copies, waits for them, and re-layouts: none -> 2.66 us  [the longest x1 1.35 us: local(): conv_weight.reshape(9, inner)]
    convert_element_type x2 -> x0, other arithmetic: 2.42 us -> none  [the longest x1 1.54 us: conv_silu(): return jax.nn.silu(summed).astype(jnp.bfloat16)]
    reduce_sum x2 -> x0, other arithmetic: 2.35 us -> none  [the longest x1 1.19 us: layer_norm(): spread = jnp.mean(center * center, axis=-1, keepdims=True)]
    unnamed x24 -> x10, local copies, waits for them, and re-layouts: 4.17 us -> 4.95 us
  transfers between devices with their start and end apart: 4 -> 0, of which waited for: 2 -> 0; matrix products, arithmetic and copies ran while one was open for 6% -> 0% of each run, Pallas kernels for 0% -> 0%
where the time goes in v2:
time: 81.4 us; the launch traced here: 81 us
  Pallas kernels  69.9 us (86%)
  local copies, waits for them, and re-layouts  9.79 us (12%)
  other arithmetic  1.35 us (2%)
    pallas_call x1, Pallas kernels, mix(): pl.pallas_call(functools.partial(scan_kernel, rows, cols), out_shape=jax....  69.9 us
    unnamed x10, local copies, waits for them, and re-layouts  4.95 us

profile of v2, /device:TPU:0, one launch (start us, length us, event | category | flops | bytes accessed | tf_op | source)
XLA Modules:
  0.0 81.0 jit_solution(11368650357460724588)
XLA Ops:
  0.0 0.0 copy-start.2
  0.0 1.3 %reshape.24.cb_ref = f32[1,384]{1,0:T(1,128)} reshape(f32[384]{0:T(512)} %param.18) | data formatting | bytes 3072 | tf_op jit(solution)/shard_map/reshape | solution.py:407
  1.3 1.2 %reshape.26.og_ref = f32[1,384]{1,0:T(1,128)} reshape(f32[384]{0:T(512)} %param.24) | data formatting | bytes 3072 | tf_op jit(solution)/shard_map/reshape | solution.py:414
  2.6 0.7 convert_element_type.3
  3.3 0.1 copy.18
  3.3 0.0 copy-start
  3.3 1.4 %reshape.23.cw_ref = bf16[9,384]{1,0:T(8,128)(2,1)} reshape(bf16[3,3,384]{2,1,0:T(4,128)(2,1)} %param.17) | data formatting | bytes 13824 | tf_op jit(solution)/shard_map/reshape | solution.py:406
  4.7 1.4 %copy.21.dtw_ref = bf16[4,12,384]{2,1,0:T(8,128)(2,1)} copy(bf16[4,12,384]{2,0,1:T(4,128)(2,1)} %param.20) | data formatting | bytes 73728 | tf_op args[7]
  6.1 0.0 copy-done.2
  6.1 0.6 multiply_bitcast_fusion.rate_ref
  6.7 0.0 copy-done
  6.7 0.8 %copy.22.ow_ref = bf16[384,192]{1,0:T(8,128)(2,1)} copy(bf16[384,192]{0,1:T(8,128)(2,1)S(1)} %copy-done) | data formatting | bytes 294912 | tf_op args[12]
  7.6 0.0 copy-start.1
  7.6 0.9 %reshape.28.tis_ref = f32[512,1]{1,0:T(8,128)} reshape(f32[32,16]{1,0:T(8,128)S(1)} %copy.18) | data formatting | bytes 4096 | tf_op jit(solution)/shard_map/reshape | solution.py:408
  8.4 0.0 copy-done.1
  8.5 1.0 %copy.20.proj_ref = bf16[4,384,44]{2,1,0:T(8,128)(2,1)} copy(bf16[4,384,44]{1,0,2:T(4,128)(2,1)S(1)} %copy-done.1) | data formatting | bytes 270336 | tf_op args[6]
  9.5 69.9 %shard_map.127 = bf16[512,192]{1,0:T(8,128)(2,1)} custom-call(bf16[512,192]{1,0:T(8,128)(2,1)} %bitcast.6, f32[1,192]{1,0:T(1,128)} %bitcast.7, bf16[192,768]{1,0:T(8,128)(2,1)} %inw_ref.1, bf16[9,384]{1,0:T(8,128)(2,1)} %reshape.23.cw_ref, f32[1,384]{1,0:T(1,128)} %reshape.24.cb_ref, f32[512,1]{1,0:T(8,128)} %reshape.28.tis_ref, ...), custom_call_target="tpu_custom_call" | custom-call | tf_op jit(solution)/shard_map/pallas_call | solution.py:347
  79.4 1.7 %copy.24 = bf16[32,16,192]{2,1,0:T(8,128)(2,1)} copy(bf16[32,16,192]{2,1,0:T(8,128)(2,1)} %bitcast.5) | data formatting | bytes 393216
Async XLA Ops:
  0.0 6.1 %copy-start.2 = (f32[4,384,16]{1,2,0:T(8,128)S(1)}, f32[4,384,16]{1,2,0:T(8,128)}, u32[]{:S(2)}) copy-start(f32[4,384,16]{1,2,0:T(8,128)} %param.22) | copy-start | bytes 294916
  3.3 3.4 %copy-start = (bf16[384,192]{0,1:T(8,128)(2,1)S(1)}, bf16[384,192]{0,1:T(8,128)(2,1)}, u32[]{:S(2)}) copy-start(bf16[384,192]{0,1:T(8,128)(2,1)} %param.25) | copy-start | bytes 442372
  7.6 0.9 %copy-start.1 = (bf16[4,384,44]{1,0,2:T(4,128)(2,1)S(1)}, bf16[4,384,44]{1,0,2:T(4,128)(2,1)}, u32[]{:S(2)}) copy-start(bf16[4,384,44]{1,0,2:T(4,128)(2,1)} %param.19) | copy-start | bytes 405508

commit v3 on v2

--- a/solution.py
+++ b/solution.py
@@ -13,6 +13,18 @@
 STAGGER = 3
 SPAN = 4
 MESH = pl.DeviceIdType.MESH
+
+
+def spread_pair(m, directions, rank, count, pk, ex):
+    source = lax.broadcasted_iota(jnp.int32, (2 * LANES, 2 * LANES), 0) % LANES
+    target = lax.broadcasted_iota(jnp.int32, (2 * LANES, 2 * LANES), 1) // LANES
+    pick = (source == target + (rank + 2 * m)).astype(jnp.bfloat16)
+    for k in directions:
+        for c in range(count // 256):
+            at = pl.ds(c * 256, 256)
+            value = jnp.dot(pk[k, at, :], pick, preferred_element_type=jnp.float32)
+            ex[k, 2 * m, at, :] = value[:, :LANES]
+            ex[k, 2 * m + 1, at, :] = value[:, LANES:]
 
 
 def spread_out(rows, cols, rank, nstate, pj, pk, ex):
@@ -36,17 +48,8 @@
             pk[k, at, :LANES] = high
             pk[k, at, LANES:] = low
 
-    source = lax.broadcasted_iota(jnp.int32, (2 * LANES, 2 * LANES), 0) % LANES
-    target = lax.broadcasted_iota(jnp.int32, (2 * LANES, 2 * LANES), 1) // LANES
-
     def pair(m, _):
-        pick = (source == target + (rank + 2 * m)).astype(jnp.bfloat16)
-        for k in range(4):
-            for c in range(count // 256):
-                at = pl.ds(c * 256, 256)
-                value = jnp.dot(pk[k, at, :], pick, preferred_element_type=jnp.float32)
-                ex[k, 2 * m, at, :] = value[:, :LANES]
-                ex[k, 2 * m + 1, at, :] = value[:, LANES:]
+        spread_pair(m, (0, 2), rank, count, pk, ex)
         return 0
 
     lax.fori_loop(0, nstate, pair, 0)
@@ -282,15 +285,22 @@
             sbuf[u] = jnp.concatenate(state, axis=0).astype(jnp.bfloat16)
             copy_of(u, device).start()
 
-    slots = max(STAGGER * (ncol - 1) + row_units, STAGGER * (nrow - 1) + col_units)
+    later = nstate if wide_refs else 0
+    slots = max(STAGGER * (ncol - 1) + row_units, STAGGER * (nrow - 1) + col_units + later)
 
     def slot(s, _):
         for k, ahead, device, size, units, first in plans:
-            q = s - STAGGER * ahead
+            q = s - STAGGER * ahead - (later if k % 2 else 0)
 
             @pl.when((q >= 0) & (q < units))
             def _():
                 unit(k, ahead, device, size, first, q)
+
+        if wide_refs:
+
+            @pl.when(s < nstate)
+            def _():
+                spread_pair(s, (1, 3), rank, count, *wide_refs)
 
         return 0
 

time: 81.4 us -> 79.6 us (0.978)
  Pallas kernels: 69.9 us -> 68.1 us
    pallas_call x1, Pallas kernels: 69.9 us -> 68.1 us  [mix(): pl.pallas_call(functools.partial(scan_kernel, rows, cols), out_shape=jax....]
where the time goes in v3:
time: 79.6 us; the launch traced here: 79.2 us
  Pallas kernels  68.1 us (86%)
  local copies, waits for them, and re-layouts  9.79 us (12%)
  other arithmetic  1.35 us (2%)
    pallas_call x1, Pallas kernels, mix(): pl.pallas_call(functools.partial(scan_kernel, rows, cols), out_shape=jax....  68.1 us
    unnamed x10, local copies, waits for them, and re-layouts  4.95 us

profile of v3, /device:TPU:0, one launch (start us, length us, event | category | flops | bytes accessed | tf_op | source)
XLA Modules:
  0.0 79.2 jit_solution(6897397344542743544)
XLA Ops:
  0.0 0.0 copy-start.2
  0.0 1.3 %reshape.24.cb_ref = f32[1,384]{1,0:T(1,128)} reshape(f32[384]{0:T(512)} %param.18) | data formatting | bytes 3072 | tf_op jit(solution)/shard_map/reshape | solution.py:417
  1.3 1.2 %reshape.26.og_ref = f32[1,384]{1,0:T(1,128)} reshape(f32[384]{0:T(512)} %param.24) | data formatting | bytes 3072 | tf_op jit(solution)/shard_map/reshape | solution.py:424
  2.6 0.7 convert_element_type.3
  3.3 0.1 copy.18
  3.3 0.0 copy-start
  3.3 1.4 %reshape.23.cw_ref = bf16[9,384]{1,0:T(8,128)(2,1)} reshape(bf16[3,3,384]{2,1,0:T(4,128)(2,1)} %param.17) | data formatting | bytes 13824 | tf_op jit(solution)/shard_map/reshape | solution.py:416
  4.7 1.4 %copy.21.dtw_ref = bf16[4,12,384]{2,1,0:T(8,128)(2,1)} copy(bf16[4,12,384]{2,0,1:T(4,128)(2,1)} %param.20) | data formatting | bytes 73728 | tf_op args[7]
  6.1 0.0 copy-done.2
  6.1 0.6 multiply_bitcast_fusion.rate_ref
  6.7 0.0 copy-done
  6.7 0.8 %copy.22.ow_ref = bf16[384,192]{1,0:T(8,128)(2,1)} copy(bf16[384,192]{0,1:T(8,128)(2,1)S(1)} %copy-done) | data formatting | bytes 294912 | tf_op args[12]
  7.6 0.0 copy-start.1
  7.6 0.9 %reshape.28.tis_ref = f32[512,1]{1,0:T(8,128)} reshape(f32[32,16]{1,0:T(8,128)S(1)} %copy.18) | data formatting | bytes 4096 | tf_op jit(solution)/shard_map/reshape | solution.py:418
  8.4 0.0 copy-done.1
  8.5 1.0 %copy.20.proj_ref = bf16[4,384,44]{2,1,0:T(8,128)(2,1)} copy(bf16[4,384,44]{1,0,2:T(4,128)(2,1)S(1)} %copy-done.1) | data formatting | bytes 270336 | tf_op args[6]
  9.5 68.1 %shard_map.127 = bf16[512,192]{1,0:T(8,128)(2,1)} custom-call(bf16[512,192]{1,0:T(8,128)(2,1)} %bitcast.6, f32[1,192]{1,0:T(1,128)} %bitcast.7, bf16[192,768]{1,0:T(8,128)(2,1)} %inw_ref.1, bf16[9,384]{1,0:T(8,128)(2,1)} %reshape.23.cw_ref, f32[1,384]{1,0:T(1,128)} %reshape.24.cb_ref, f32[512,1]{1,0:T(8,128)} %reshape.28.tis_ref, ...), custom_call_target="tpu_custom_call" | custom-call | tf_op jit(solution)/shard_map/pallas_call | solution.py:357
  77.6 1.7 %copy.24 = bf16[32,16,192]{2,1,0:T(8,128)(2,1)} copy(bf16[32,16,192]{2,1,0:T(8,128)(2,1)} %bitcast.5) | data formatting | bytes 393216
Async XLA Ops:
  0.0 6.1 %copy-start.2 = (f32[4,384,16]{1,2,0:T(8,128)S(1)}, f32[4,384,16]{1,2,0:T(8,128)}, u32[]{:S(2)}) copy-start(f32[4,384,16]{1,2,0:T(8,128)} %param.22) | copy-start | bytes 294916
  3.3 3.4 %copy-start = (bf16[384,192]{0,1:T(8,128)(2,1)S(1)}, bf16[384,192]{0,1:T(8,128)(2,1)}, u32[]{:S(2)}) copy-start(bf16[384,192]{0,1:T(8,128)(2,1)} %param.25) | copy-start | bytes 442372
  7.6 0.9 %copy-start.1 = (bf16[4,384,44]{1,0,2:T(4,128)(2,1)S(1)}, bf16[4,384,44]{1,0,2:T(4,128)(2,1)}, u32[]{:S(2)}) copy-start(bf16[4,384,44]{1,0,2:T(4,128)(2,1)} %param.19) | copy-start | bytes 405508
